TPU v7x, 256 devices: a whole 4x4x8 slice. The times are simulated.
256 devices in a mesh: rows: 32 (over x, z_hi, core), feat: 8 (over y, z_lo).
Axes of the slice: x: 4, y: 4, z: 8 (z_hi: 4, z_lo: 2; z = z_hi * 2 + z_lo), core: 2. Of those that a mesh axis runs over, the one named last changes fastest.
Arguments:
- data: bfloat16 [196608, 1024], P(('rows', 'feat')), may hold values from -6 to 6
- rotation: bfloat16 [1024, 1024], P(None, 'feat'), may hold values from -0.1875 to 0.1875
- codebook: bfloat16 [256, 1024], P(None, 'feat'), may hold values from -5 to 5
Outputs:
- new_codebook: float32 [256, 1024], P(None, 'feat')
- counts: float32 [64, 256], P('feat')
- cross: float32 [1024, 1024], P('rows', 'feat')
All inputs are finite; a program needn't handle non-finite values.
Results may differ from a plain program's by a relative error of at most 0.0029.
Values may be sent and summed in bfloat16 or wider, within the bound.
No kernel may reach another device: no remote copies, remote signals or barrier semaphores. Data moves between devices by JAX's collectives and lax.ppermute only.
A program may use at most 64 MiB of HBM per device.

v0:
```python
import jax
import jax.numpy as jnp
from jax import lax
from jax.sharding import PartitionSpec as P

D = 1024
SUB = 64
inverse_temp = 0.5


def assign(grouped, code_local):
    rows_all, width = grouped.shape
    sub_width = D // SUB
    local_subs = width // sub_width
    words = code_local.shape[0]
    block = 1024
    codes = code_local.reshape(words, local_subs, sub_width)
    code_wide = code_local.astype(jnp.float32).reshape(words, local_subs, sub_width)
    squares = jnp.sum(code_wide * code_wide, axis=-1).T[:, None, :]

    def step(carry, piece):
        numer, counted = carry
        values = piece.reshape(block, local_subs, sub_width)
        dots = jnp.einsum("nsd,ksd->snk", values, codes, preferred_element_type=jnp.float32)
        logits = inverse_temp * (2.0 * dots - squares)
        weights = jax.nn.softmax(logits, axis=-1)
        weights_b = weights.astype(jnp.bfloat16)
        numer = numer + jnp.einsum(
            "snk,nsd->ksd", weights_b, values, preferred_element_type=jnp.float32
        ).reshape(words, width)
        counted = counted + jnp.sum(weights, axis=1)
        rebuilt = jnp.einsum("snk,ksd->nsd", weights_b, codes, preferred_element_type=jnp.float32)
        return ((numer, counted), rebuilt.reshape(block, width).astype(jnp.bfloat16))

    start = (jnp.zeros((words, width), jnp.float32), jnp.zeros((local_subs, words), jnp.float32))
    (numer, counted), rebuilt = lax.scan(
        step, start, grouped.reshape(rows_all // block, block, width)
    )
    return (numer, counted, rebuilt.reshape(rows_all, width))


def local(data, rotation, codebook):
    width = D
    full_rotation = lax.all_gather(rotation, "feat", axis=1, tiled=True)
    own = jnp.dot(data, full_rotation, preferred_element_type=jnp.float32).astype(jnp.bfloat16)
    grouped = lax.all_to_all(own, "feat", split_axis=1, concat_axis=0, tiled=True)
    numer, counted, rebuilt = assign(grouped, codebook)
    back = lax.all_to_all(rebuilt, "feat", split_axis=0, concat_axis=1, tiled=True)
    term = lax.dot_general(data, back, (((0,), (0,)), ((), ())), preferred_element_type=jnp.float32)
    n_rows = lax.axis_size("rows")
    n_feat = lax.axis_size("feat")
    ordered = term.reshape(n_rows, width // n_rows, n_feat, width // n_feat)
    ordered = ordered.transpose(0, 2, 1, 3).reshape(
        n_rows * n_feat * (width // n_rows), width // n_feat
    )
    cross = lax.psum_scatter(ordered, ("rows", "feat"), scatter_dimension=0, tiled=True)
    total_numer, total_counts = lax.psum((numer, counted), "rows")
    per_column = jnp.repeat(total_counts.T, D // SUB, axis=1)
    new_codebook = (total_numer + codebook.astype(jnp.float32)) / (per_column + 1.0)
    return (new_codebook, total_counts, cross)


def solution(mesh):
    in_specs = (P(("rows", "feat"), None), P(None, "feat"), P(None, "feat"))
    out_specs = (P(None, "feat"), P("feat", None), P("rows", "feat"))
    return jax.shard_map(local, mesh=mesh, in_specs=in_specs, out_specs=out_specs, check_vma=False)
```

profile of v0, /device:TPU:0, one launch (start us, length us, event | category | flops | bytes accessed | tf_op | source)
XLA Modules:
  0.0 1752.2 jit_solution(6497450159070339519)
XLA Ops:
  7.9 57.3 %all-gather.2.cloned.1.call-done = bf16[1024,1024]{1,0:T(8,128)(2,1)} async-done(((bf16[1024,128]{1,0:T(8,128)(2,1)}), bf16[1024,1024]{1,0:T(8,128)(2,1)}) %all-gather.2.cloned.1.call-update) | async-done | bytes 2097168 | tf_op jit(solution)/shard_map/all_gather | solution.py:44
  65.3 3.4 fusion.11
  70.1 4.4 all-to-all-start
  74.7 20.2 %all-to-all-done = bf16[768,8,128]{2,0,1:T(8,128)(2,1)} async-done(((bf16[768,8,128]{2,0,1:T(8,128)(2,1)}), bf16[768,8,128]{2,0,1:T(8,128)(2,1)}, u32[]{:S(2)}, u32[]{:S(2)}) %all-to-all-start) | async-done | bytes 1572896 | tf_op jit(solution)/shard_map/all_to_all | solution.py:46
  94.9 106.3 %while.15 = (s32[]{:T(128)}, f32[256,128]{0,1:T(8,128)S(1)}, f32[8,256]{1,0:T(8,128)S(1)}, bf16[6,1024,128]{2,1,0:T(8,128)(2,1)}, bf16[6,1024,128]{2,1,0:T(8,128...) while((s32[]{:T(128)}, f32[256,128]{0,1:T(8,128)S(1)}, ...), condition=%wide.region_5.6_spmd.clone, body=%wide.region_1.5_spmd.clone.sunk | while | flops 218302720 | bytes 49783428 | solution.py:36
  96.0 5.5 fusion.42
  101.5 4.2 fusion.43
  113.7 5.5 fusion.42
  119.2 4.2 fusion.43
  131.4 5.5 fusion.42
  136.9 4.2 fusion.43
  149.2 5.5 fusion.42
  154.6 4.2 fusion.43
  166.9 5.5 fusion.42
  172.4 4.2 fusion.43
  184.6 5.5 fusion.42
  190.1 4.2 fusion.43
  201.2 3.6 all-to-all-start.1
  205.6 19.5 %all-to-all-done.1 = bf16[8,768,128]{2,1,0:T(8,128)(2,1)S(1)} async-done(((bf16[8,768,128]{2,1,0:T(8,128)(2,1)}), bf16[8,768,128]{2,1,0:T(8,128)(2,1)S(1)}, u32[]{:S(2)}, u32[]{:S(2)}) %all-to-all-start.1) | async-done | bytes 1572896 | tf_op jit(solution)/shard_map/all_to_all | solution.py:48
  226.6 5.1 convolution_bitcast_fusion
  231.8 5.4 copy.30
  243.6 70.9 %psum.15 = f32[8,256]{1,0:T(8,128)S(1)} all-reduce(f32[8,256]{1,0:T(8,128)S(1)} %get-tuple-element.43), channel_id=1, replica_groups=mesh['rows'=32,'feat'=8] {'rows'}, use_global_device_ids=true, to_apply=%region_7.8 | all-reduce | flops 2048 | bytes 16384 | tf_op jit(solution)/shard_map/psum | solution.py:57
  314.5 155.2 %all-reduce.2.cloned.1.call-done = f32[256,128]{0,1:T(8,128)} async-done(((f32[256,128]{0,1:T(8,128)}), f32[256,128]{0,1:T(8,128)}) %all-reduce.2.cloned.1.call-update) | async-done | bytes 131088 | tf_op jit(solution)/shard_map/psum | solution.py:57
  471.4 1274.3 %reduce-scatter.2.cloned.1.call-done = f32[32,128]{1,0:T(8,128)} async-done(((f32[8192,128]{1,0:T(8,128)}), f32[32,128]{1,0:T(8,128)}) %reduce-scatter.2.cloned.1.call-update) | async-done | bytes 16400 | tf_op jit(solution)/shard_map/reduce_scatter | solution.py:56
  (87 shorter events, 60.9 us)
Async XLA Ops:
  7.2 58.1 %copy-start = (bf16[768,1024]{1,0:T(8,128)(2,1)S(1)}, bf16[768,1024]{1,0:T(8,128)(2,1)}, u32[]{:S(2)}) copy-start(bf16[768,1024]{1,0:T(8,128)(2,1)} %param.5) | copy-start | bytes 4718596
  7.2 58.1 %all-gather.2.cloned.1.call-start = ((), (), s32[]{:S(2)}) async-start(), calls=%async_computation.3 | async-start | bytes 2359296 | tf_op jit(solution)/shard_map/all_gather | solution.py:44
  68.6 5.9 copy-start.3
  70.1 24.8 %all-to-all-start = ((bf16[768,8,128]{2,0,1:T(8,128)(2,1)}), bf16[768,8,128]{2,0,1:T(8,128)(2,1)}, u32[]{:S(2)}, u32[]{:S(2)}) async-start(bf16[768,8,128]{2,0,1:T(8,128)(2,1)} %bitcast.50), calls=%async_computation | async-start | bytes 3145728 | tf_op jit(solution)/shard_map/all_to_all | solution.py:46
  105.7 1.9 copy-start.1
  123.4 1.9 copy-start.1
  141.1 1.9 copy-start.1
  158.8 1.9 copy-start.1
  176.6 1.9 copy-start.1
  194.3 1.9 copy-start.1
  201.2 3.6 copy-start.2
  201.2 23.9 %all-to-all-start.1 = ((bf16[8,768,128]{2,1,0:T(8,128)(2,1)}), bf16[8,768,128]{2,1,0:T(8,128)(2,1)S(1)}, u32[]{:S(2)}, u32[]{:S(2)}) async-start(bf16[8,768,128]{2,1,0:T(8,128)(2,1)} %bitcast.81), calls=%async_computation.1 | async-start | bytes 3145728 | tf_op jit(solution)/shard_map/all_to_all | solution.py:48
  204.8 264.9 %all-reduce.2.cloned.1.call-start = ((), (), s32[]{:S(2)}) async-start(), calls=%async_computation.4 | async-start | bytes 262144 | tf_op jit(solution)/shard_map/psum | solution.py:57
  205.5 1540.1 %reduce-scatter.2.cloned.1.call-start = ((), (), s32[]{:S(2)}) async-start(), calls=%async_computation.5 | async-start | bytes 4210688 | tf_op jit(solution)/shard_map/reduce_scatter | solution.py:56
  314.4 1431.2 %copy-start.4 = (f32[8,256]{1,0:T(8,128)}, f32[8,256]{1,0:T(8,128)S(1)}, u32[]{:S(2)}) copy-start(f32[8,256]{1,0:T(8,128)S(1)} %psum.15) | copy-start | bytes 24580
Sparse Core Ops, SparseCore 0:
  9.7 55.4 all-gather.1
  208.8 260.8 all-reduce.1
  472.9 1272.7 reduce-scatter.1
where the time goes:
time: 1750 us
  waiting for transfers between devices  1530 us (87%)
  blocking collectives  70.9 us (4%)
  matrix products  65.5 us (4%)
  local copies, waits for them, and re-layouts  39.4 us (2%)
  other arithmetic  26.3 us (2%)
    reduce_scatter x1, waiting for transfers between devices, local(): lax.psum_scatter(ordered, ('rows', 'feat'), scatter_dimension=0, tiled=True)  1270 us
    psum x1, waiting for transfers between devices, local(): total_numer, total_counts = lax.psum((numer, counted), 'rows')  155 us
    psum x1, blocking collectives, local(): total_numer, total_counts = lax.psum((numer, counted), 'rows')  70.9 us
    all_gather x1, waiting for transfers between devices, local(): full_rotation = lax.all_gather(rotation, 'feat', axis=1, tiled=True)  57.3 us
  transfers between devices with their start and end apart: 5, of which 5 were waited for; matrix products, arithmetic and copies ran while one was open for 1% of the time, Pallas kernels for 0%

commit v1 on v0

--- a/solution.py
+++ b/solution.py
@@ -41,7 +41,9 @@
 
 def local(data, rotation, codebook):
     width = D
-    full_rotation = lax.all_gather(rotation, "feat", axis=1, tiled=True)
+    full_rotation = jnp.concatenate(
+        lax.all_to_all(jnp.stack([rotation] * lax.axis_size("feat")), "feat", 0, 0), axis=1
+    )
     own = jnp.dot(data, full_rotation, preferred_element_type=jnp.float32).astype(jnp.bfloat16)
     grouped = lax.all_to_all(own, "feat", split_axis=1, concat_axis=0, tiled=True)
     numer, counted, rebuilt = assign(grouped, codebook)

time: 1750 us -> 1500 us (0.86)
  waiting for transfers between devices: 1530 us -> 1240 us
  blocking collectives: 70.9 us -> 107 us
    reduce_scatter x1, waiting for transfers between devices: 1270 us -> 1050 us  [local(): lax.psum_scatter(ordered, ('rows', 'feat'), scatter_dimension=0, tiled=True)]
    all_gather x1 -> x0, waiting for transfers between devices: 57.3 us -> none  [local(): full_rotation = lax.all_gather(rotation, 'feat', axis=1, tiled=True)]
    all_to_all x0 -> x1, blocking collectives: none -> 31.1 us  [local(): lax.all_to_all(jnp.stack([rotation] * lax.axis_size('feat')), 'feat', 0, 0)]
  transfers between devices with their start and end apart: 5 -> 4, of which waited for: 5 -> 4; matrix products, arithmetic and copies ran while one was open for 1% -> 1% of each run, Pallas kernels for 0% -> 0%
where the time goes in v1:
time: 1500 us
  waiting for transfers between devices  1240 us (83%)
  blocking collectives  107 us (7%)
  matrix products  64 us (4%)
  local copies, waits for them, and re-layouts  40.7 us (3%)
  other arithmetic  26.3 us (2%)
  between operations  15.6 us (1%)
    reduce_scatter x1, waiting for transfers between devices, local(): lax.psum_scatter(ordered, ('rows', 'feat'), scatter_dimension=0, tiled=True)  1050 us
    psum x1, waiting for transfers between devices, local(): total_numer, total_counts = lax.psum((numer, counted), 'rows')  153 us
    psum x1, blocking collectives, local(): total_numer, total_counts = lax.psum((numer, counted), 'rows')  75.8 us
    sub x6, matrix products, step(): weights = jax.nn.softmax(logits, axis=-1)  32.9 us
    all_to_all x1, blocking collectives, local(): lax.all_to_all(jnp.stack([rotation] * lax.axis_size('feat')), 'feat', 0, 0)  31.1 us
  transfers between devices with their start and end apart: 4, of which 4 were waited for; matrix products, arithmetic and copies ran while one was open for 1% of the time, Pallas kernels for 0%

profile of v1, /device:TPU:0, one launch (start us, length us, event | category | flops | bytes accessed | tf_op | source)
XLA Modules:
  0.0 1503.0 jit_solution(2880537556014882394)
XLA Ops:
  9.5 31.1 %all_to_all.40 = bf16[8,1024,128]{1,2,0:T(8,128)(2,1)S(1)} all-to-all(bf16[8,1024,128]{1,2,0:T(8,128)(2,1)S(1)} %stack.2), channel_id=1, replica_groups=mesh['rows'=32,'feat'=8] {'feat'}, dimensions={0} | all-to-all | bytes 4194304 | tf_op jit(solution)/shard_map/all_to_all | solution.py:45
  43.9 4.3 all-to-all-start.1
  48.4 20.2 %all-to-all-done.1 = bf16[768,8,128]{2,0,1:T(8,128)(2,1)} async-done(((bf16[768,8,128]{2,0,1:T(8,128)(2,1)}), bf16[768,8,128]{2,0,1:T(8,128)(2,1)}, u32[]{:S(2)}, u32[]{:S(2)}) %all-to-all-start.1) | async-done | bytes 1572896 | tf_op jit(solution)/shard_map/all_to_all | solution.py:48
  68.6 106.2 %while.15 = (s32[]{:T(128)}, f32[256,128]{0,1:T(8,128)S(1)}, f32[8,256]{1,0:T(8,128)S(1)}, bf16[6,1024,128]{2,1,0:T(8,128)(2,1)}, bf16[6,1024,128]{2,1,0:T(8,128...) while((s32[]{:T(128)}, f32[256,128]{0,1:T(8,128)S(1)}, ...), condition=%wide.region_5.6_spmd.clone, body=%wide.region_1.5_spmd.clone.sunk | while | flops 218302720 | bytes 49783428 | solution.py:36
  69.8 5.5 fusion.42
  75.2 4.2 fusion.43
  87.5 5.5 fusion.42
  92.9 4.2 fusion.43
  105.2 5.5 fusion.42
  110.7 4.2 fusion.43
  122.9 5.5 fusion.42
  128.4 4.2 fusion.43
  140.6 5.5 fusion.42
  146.1 4.2 fusion.43
  158.3 5.5 fusion.42
  163.8 4.2 fusion.43
  174.9 3.6 all-to-all-start.2
  179.3 19.7 %all-to-all-done.2 = bf16[8,768,128]{2,1,0:T(8,128)(2,1)S(1)} async-done(((bf16[8,768,128]{2,1,0:T(8,128)(2,1)}), bf16[8,768,128]{2,1,0:T(8,128)(2,1)S(1)}, u32[]{:S(2)}, u32[]{:S(2)}) %all-to-all-start.2) | async-done | bytes 1572896 | tf_op jit(solution)/shard_map/all_to_all | solution.py:50
  200.6 5.1 convolution_bitcast_fusion
  205.7 5.4 copy.32
  211.0 3.2 copy.41
  217.4 75.8 %psum.15 = f32[8,256]{1,0:T(8,128)S(1)} all-reduce(f32[8,256]{1,0:T(8,128)S(1)} %get-tuple-element.43), channel_id=1, replica_groups=mesh['rows'=32,'feat'=8] {'rows'}, use_global_device_ids=true, to_apply=%region_7.8 | all-reduce | flops 2048 | bytes 16384 | tf_op jit(solution)/shard_map/psum | solution.py:59
  293.3 153.0 %all-reduce.2.cloned.1.call-done = f32[256,128]{0,1:T(8,128)} async-done(((f32[256,128]{0,1:T(8,128)}), f32[256,128]{0,1:T(8,128)}) %all-reduce.2.cloned.1.call-update) | async-done | bytes 131088 | tf_op jit(solution)/shard_map/psum | solution.py:59
  447.9 1047.6 %reduce-scatter.2.cloned.1.call-done = f32[32,128]{1,0:T(8,128)} async-done(((f32[8192,128]{1,0:T(8,128)}), f32[32,128]{1,0:T(8,128)}) %reduce-scatter.2.cloned.1.call-update) | async-done | bytes 16400 | tf_op jit(solution)/shard_map/reduce_scatter | solution.py:58
  (87 shorter events, 60.1 us)
Async XLA Ops:
  8.0 32.6 %copy-start = (bf16[768,1024]{1,0:T(8,128)(2,1)S(1)}, bf16[768,1024]{1,0:T(8,128)(2,1)}, u32[]{:S(2)}) copy-start(bf16[768,1024]{1,0:T(8,128)(2,1)} %param.5) | copy-start | bytes 4718596
  42.5 5.8 copy-start.3
  43.9 24.7 %all-to-all-start.1 = ((bf16[768,8,128]{2,0,1:T(8,128)(2,1)}), bf16[768,8,128]{2,0,1:T(8,128)(2,1)}, u32[]{:S(2)}, u32[]{:S(2)}) async-start(bf16[768,8,128]{2,0,1:T(8,128)(2,1)} %bitcast.53), calls=%async_computation.1 | async-start | bytes 3145728 | tf_op jit(solution)/shard_map/all_to_all | solution.py:48
  79.4 1.9 copy-start.1
  97.1 1.9 copy-start.1
  114.8 1.9 copy-start.1
  132.5 1.9 copy-start.1
  150.3 1.9 copy-start.1
  168.0 1.9 copy-start.1
  174.9 3.6 copy-start.2
  174.9 24.1 %all-to-all-start.2 = ((bf16[8,768,128]{2,1,0:T(8,128)(2,1)}), bf16[8,768,128]{2,1,0:T(8,128)(2,1)S(1)}, u32[]{:S(2)}, u32[]{:S(2)}) async-start(bf16[8,768,128]{2,1,0:T(8,128)(2,1)} %bitcast.85), calls=%async_computation.2 | async-start | bytes 3145728 | tf_op jit(solution)/shard_map/all_to_all | solution.py:50
  178.5 267.8 %all-reduce.2.cloned.1.call-start = ((), (), s32[]{:S(2)}) async-start(), calls=%async_computation.4 | async-start | bytes 262144 | tf_op jit(solution)/shard_map/psum | solution.py:59
  179.2 1316.3 %reduce-scatter.2.cloned.1.call-start = ((), (), s32[]{:S(2)}) async-start(), calls=%async_computation.5 | async-start | bytes 4210688 | tf_op jit(solution)/shard_map/reduce_scatter | solution.py:58
  293.2 1202.3 %copy-start.4 = (f32[8,256]{1,0:T(8,128)}, f32[8,256]{1,0:T(8,128)S(1)}, u32[]{:S(2)}) copy-start(f32[8,256]{1,0:T(8,128)S(1)} %psum.15) | copy-start | bytes 24580
Sparse Core Ops, SparseCore 0:
  182.5 263.6 all-reduce.1
Sparse Core Ops, SparseCore 1:
  217.5 1278.0 reduce-scatter.1
